TPU v7x, 32 devices: a whole 2x2x4 slice. The times are simulated.
32 devices in a mesh: groups: 2 (over y), cache: 4 (over z), heads: 2 (over x), pair: 2 (over core).
Axes of the slice: x: 2, y: 2, z: 4, core: 2. Of those that a mesh axis runs over, the one named last changes fastest.
Arguments:
- queries: bfloat16 [3328, 8192], P(('groups', 'cache'), ('heads', 'pair')), parts along dimension 0, may hold values from -6 to 6
- new_keys: bfloat16 [3328, 1024], P(('groups', 'cache'), ('heads', 'pair')), parts along dimension 0, may hold values from -6 to 6
- new_values: bfloat16 [3328, 1024], P(('groups', 'cache'), ('heads', 'pair')), parts along dimension 0, may hold values from -6 to 6
- cache_keys: bfloat16 [64, 256, 1024], P(('groups', 'cache', 'pair'), None, 'heads'), parts along dimension 0, may hold values from -6 to 6
- cache_values: bfloat16 [64, 256, 1024], P(('groups', 'cache', 'pair'), None, 'heads'), parts along dimension 0, may hold values from -6 to 6
- request_pass: int32 [16, 8], P(('groups', 'cache')), parts along dimension 0, may hold values from 0 to 31, as said below
- rec_block: int32 [16, 1], P(('groups', 'cache')), parts along dimension 0, may hold values from 0 to 15, as said below
- passage_slot: int32 [64], P('groups'), parts along dimension 0, may hold values from 0 to 31, as said below
Outputs:
- attention: bfloat16 [3328, 8192], P(('groups', 'cache'), ('heads', 'pair')), parts along dimension 0
There are 2 independent parts, one for each index of `groups`. A program takes and returns all parts, laid end to end along the dimension named above; each array names one. Nothing has to cross between parts.
Inputs may be any that keep to these rules, and one draw needn't show every extreme that they name: `request_pass`: the 16 passages named by the requests of one index of cache are distinct. An owner of slot s is the device s // 4 of cache and pair together; of those passages every owner holds 2 or 1, and some owner exactly 2. `passage_slot`: A permutation. `rec_block`: within each request distinct and increasing.
All inputs are finite; a program needn't handle non-finite values.
Results may differ from a plain program's by a relative error of at most 0.0038.
Values may be sent and summed in bfloat16 or wider, within the bound.
A program may use at most 64 MiB of HBM per device.

v0:
```python
import math

import jax
import jax.numpy as jnp
from jax import lax
from jax.sharding import PartitionSpec as P

HD = 128
BLOCK = 128


def rank_within(owner_rows):
    ref_total = owner_rows.shape[-1]
    same_owner = owner_rows[..., :, None] == owner_rows[..., None, :]
    earlier = jnp.arange(ref_total)[None, :] < jnp.arange(ref_total)[:, None]
    return jnp.sum(same_owner & earlier, axis=-1)


def attend_block(query_rows, key_rows, value_rows, query_pos):
    key_scale = 1.0 / math.sqrt(query_rows.shape[-1])
    scores = (
        jnp.einsum("rd,kd->rk", query_rows, key_rows, preferred_element_type=jnp.float32)
        * key_scale
    )
    key_pos = jnp.arange(key_rows.shape[0], dtype=jnp.int32)
    scores = jnp.where(key_pos[None, :] <= query_pos[:, None], scores, -jnp.inf)
    row_max = jnp.max(scores, axis=1, keepdims=True)
    weights = jnp.exp(scores - row_max)
    totals = jnp.sum(weights, axis=1, keepdims=True)
    mixed_rows = jnp.dot(
        weights.astype(jnp.bfloat16), value_rows, preferred_element_type=jnp.float32
    )
    return (mixed_rows / totals).astype(jnp.bfloat16)


def on_device(
    queries, new_keys, new_values, cache_keys, cache_values, request_pass, rec_block, passage_slot
):
    local_requests, per_request = request_pass.shape
    ref_total = local_requests * per_request
    cache_count = lax.axis_size("cache")
    pair_count = lax.axis_size("pair")
    owner_total = cache_count * pair_count
    slot_room = max(1, (ref_total + owner_total - 1) // owner_total)
    pass_dev, pass_len, cache_width = cache_keys.shape
    kv_width = cache_width // pair_count
    everyone = lax.all_gather(request_pass, "cache", axis=0, tiled=True).reshape(
        cache_count, ref_total
    )
    slots_all = jnp.take(passage_slot, everyone)
    owner_all = slots_all // pass_dev
    local_all = slots_all % pass_dev
    rank_all = rank_within(owner_all)
    myself = lax.axis_index("cache") * pair_count + lax.axis_index("pair")
    wanted = (owner_all == myself)[:, :, None] & (
        rank_all[:, :, None] == jnp.arange(slot_room, dtype=jnp.int32)[None, None, :]
    )
    picked = jnp.sum(jnp.where(wanted, local_all[:, :, None] + 1, 0), axis=1) - 1
    safe_pick = jnp.clip(picked, 0, pass_dev - 1)
    chosen = jnp.stack((cache_keys[safe_pick], cache_values[safe_pick]), axis=2)
    chosen = jnp.where((picked >= 0)[:, :, None, None, None], chosen, jnp.zeros((), jnp.bfloat16))
    chosen = chosen.reshape(cache_count, slot_room, 2, pass_len, pair_count, kv_width)
    outgoing = jnp.transpose(chosen, (0, 4, 1, 2, 3, 5))
    arrived = lax.all_to_all(
        outgoing.reshape(owner_total, slot_room, 2, pass_len, kv_width),
        ("cache", "pair"),
        split_axis=0,
        concat_axis=0,
        tiled=True,
    )
    local_slots = jnp.take(passage_slot, request_pass.reshape(ref_total))
    source_owner = local_slots // pass_dev
    source_rank = rank_within(source_owner)
    fetched = arrived[source_owner, source_rank].reshape(
        local_requests, per_request, 2, pass_len, kv_width
    )
    row_count = queries.shape[0] // local_requests

    def one_request(inputs):
        request_queries, fresh_keys, fresh_values, blocks, fetched_req = inputs
        recomputed = blocks.shape[0]
        context = per_request * pass_len
        context_keys = fetched_req[:, 0].reshape(context, kv_width)
        context_values = fetched_req[:, 1].reshape(context, kv_width)
        start_row = blocks[0] * BLOCK
        context_keys = lax.dynamic_update_slice(
            context_keys, fresh_keys[0:BLOCK], (start_row, jnp.int32(0))
        )
        context_values = lax.dynamic_update_slice(
            context_values, fresh_values[0:BLOCK], (start_row, jnp.int32(0))
        )
        question = row_count - recomputed * BLOCK
        key_rows = jnp.concatenate((context_keys, fresh_keys[recomputed * BLOCK :]), axis=0)
        value_rows = jnp.concatenate((context_values, fresh_values[recomputed * BLOCK :]), axis=0)
        block_pos = (blocks[:, None] * BLOCK + jnp.arange(BLOCK, dtype=jnp.int32)[None, :]).reshape(
            -1
        )
        query_pos = jnp.concatenate((block_pos, context + jnp.arange(question, dtype=jnp.int32)))
        kv_heads = kv_width // HD
        group_size = request_queries.shape[1] // kv_width
        arranged = request_queries.reshape(row_count, kv_heads, group_size, HD).transpose(
            1, 2, 0, 3
        )
        tiled_pos = jnp.tile(query_pos, 4)
        outputs = []
        for kv_head in range(kv_heads):
            head_keys = key_rows.reshape(-1, kv_heads, HD)[:, kv_head]
            head_values = value_rows.reshape(-1, kv_heads, HD)[:, kv_head]
            blocked = arranged[kv_head].reshape(group_size // 4, 4 * row_count, HD)
            attended = lax.map(
                lambda block_query: attend_block(block_query, head_keys, head_values, tiled_pos),
                blocked,
            )
            outputs.append(attended.reshape(group_size, row_count, HD))
        joined = jnp.stack(outputs).transpose(2, 0, 1, 3)
        return joined.reshape(row_count, kv_heads * group_size * HD)

    results = lax.map(
        one_request,
        (
            queries.reshape(local_requests, row_count, queries.shape[1]),
            new_keys.reshape(local_requests, row_count, kv_width),
            new_values.reshape(local_requests, row_count, kv_width),
            rec_block,
            fetched,
        ),
    )
    return results.reshape(queries.shape)


def solution(mesh):
    return jax.shard_map(
        on_device,
        mesh=mesh,
        in_specs=(
            P(("groups", "cache"), ("heads", "pair")),
            P(("groups", "cache"), ("heads", "pair")),
            P(("groups", "cache"), ("heads", "pair")),
            P(("groups", "cache", "pair"), None, "heads"),
            P(("groups", "cache", "pair"), None, "heads"),
            P(("groups", "cache"), None),
            P(("groups", "cache"), None),
            P("groups"),
        ),
        out_specs=P(("groups", "cache"), ("heads", "pair")),
        check_vma=False,
    )
```

profile of v0, /device:TPU:0, one launch (start us, length us, event | category | flops | bytes accessed | tf_op | source)
XLA Modules:
  0.0 200.0 jit_solution(11152880503902789940)
XLA Ops:
  0.0 13.0 %all-gather = s32[4,2,8]{2,1,0:T(2,128)S(1)} all-gather(s32[1,2,8]{2,1,0:T(2,128)} %bitcast.157), channel_id=1, replica_groups=mesh['groups'=2,'cache'=4,'heads'=2,'pair'=2] {'cache'}, dimensions={0}, use_global_device_ids=true | all-gather | bytes 320 | tf_op jit(solution)/shard_map/all_gather | solution.py:47
  13.2 1.4 gather_fusion
  16.1 3.3 %gather_fusion.2 = bf16[8,256,512]{2,1,0:T(8,128)(2,1)} fusion(bf16[4,256,512]{2,1,0:T(8,128)(2,1)} %param.18, s32[1024]{0:T(1024)S(1)} %pad_clamp_fusion.1), kind=kCustom, calls=%fused_computation.2 | custom fusion | bytes 4194336 | tf_op jit(solution)/shard_map/gather | solution.py:60
  19.4 1.8 maximum_select_fusion
  22.2 2.4 %copy.98 = bf16[8,2,2,256,256]{4,3,1,2,0:T(8,128)(2,1)} copy(bf16[8,2,2,256,256]{4,3,2,1,0:T(8,128)(2,1)S(1)} %bitcast.149) | data formatting | bytes 8388608 | tf_op jit(solution)/shard_map/reshape | solution.py:65
  24.6 4.9 %all-to-all-start = ((bf16[8,2,2,256,256]{4,3,1,2,0:T(8,128)(2,1)}), bf16[8,2,2,256,256]{4,3,1,2,0:T(8,128)(2,1)}, u32[]{:S(2)}, u32[]{:S(2)}) async-start(bf16[8,2,2,256,256]{4,3,1,2,0:T(8,128)(2,1)} %copy.98), calls=%async_computation | async-start | bytes 8388608 | tf_op jit(solution)/shard_map/all_to_all | solution.py:64
  30.5 92.7 %all-to-all-done = bf16[8,2,2,256,256]{4,3,1,2,0:T(8,128)(2,1)} async-done(((bf16[8,2,2,256,256]{4,3,1,2,0:T(8,128)(2,1)}), bf16[8,2,2,256,256]{4,3,1,2,0:T(8,128)(2,1)}, u32[]{:S(2)}, u32[]{:S(2)}) %all-to-all-start) | async-done | bytes 4194336 | tf_op jit(solution)/shard_map/all_to_all | solution.py:64
  123.3 4.9 %gather_fusion.4 = bf16[16,2,256,256]{3,2,1,0:T(8,128)(2,1)} fusion(bf16[8,2,2,256,256]{4,3,1,2,0:T(8,128)(2,1)} %all-to-all-done, s32[16]{0:T(128)S(1)} %fusion.58), kind=kCustom, calls=%fused_computation.4 | custom fusion | bytes 8388736 | tf_op jit(solution)/shard_map/gather | solution.py:74
  128.2 70.6 %while.34 = (s32[]{:T(128)}, bf16[2,208,2048]{2,1,0:T(8,128)(2,1)}, bf16[2,208,2048]{2,1,0:T(8,128)(2,1)}, bf16[2,8,2,256,256]{4,3,2,1,0:T(8,128)(2,1)}, bf16[2,...) while((s32[]{:T(128)}, bf16[2,208,2048]{2,1,0:T(8,128)(2,1)}, ...), condition=%wide.region_12.13_spmd, body=%wide.region_3.12_spmd.sunk | while | flops 1846523136 | bytes 82808904 | solution.py:118
  131.5 1.7 dynamic-slice_bitcast_fusion.5
  139.6 10.3 %while.36 = (s32[]{:T(128)}, bf16[2,832,128]{2,1,0:T(8,128)(2,1)S(1)}, bf16[2,832,128]{2,1,0:T(8,128)(2,1)S(1)}, bf16[2128,128]{1,0:T(8,128)(2,1)}, bf16[2128,12...) while((s32[]{:T(128)}, bf16[2,832,128]{2,1,0:T(8,128)(2,1)S(1)}, ...), condition=%wide.region_7.7_spmd.clone, body=%wide.region_4.6_spmd.clone.sunk | while | flops 920869248 | bytes 22954388 | solution.py:110
  139.7 2.6 %fusion.101 = (f32[832]{0:T(1024)S(1)}, f32[832,2128]{1,0:T(8,128)S(1)}) fusion(bf16[2128,128]{1,0:T(8,128)(2,1)} %get-tuple-element.499, bf16[2,832,128]{2,1,0:T(8,128)(2,1)S(1)} %get-tuple-element.498, s32[]{:T(128)} %get-tuple-element.489, s32[832]{0:T(1024)S(1)} %le.127), kind=kOutput, calls=%fused_computation.108.clone.1 | convolution fusion | flops 460328128 | bytes 7847172 | tf_op jit(solution)/shard_map/while/body/eval_jaxpr/while/body/eval_jaxpr/rd,kd->rk/dot_general | solution.py:22
  144.8 2.6 %fusion.101 = (f32[832]{0:T(1024)S(1)}, f32[832,2128]{1,0:T(8,128)S(1)}) fusion(bf16[2128,128]{1,0:T(8,128)(2,1)} %get-tuple-element.499, bf16[2,832,128]{2,1,0:T(8,128)(2,1)S(1)} %get-tuple-element.498, s32[]{:T(128)} %get-tuple-element.489, s32[832]{0:T(1024)S(1)} %le.127), kind=kOutput, calls=%fused_computation.108.clone.1 | convolution fusion | flops 460328128 | bytes 7847172 | tf_op jit(solution)/shard_map/while/body/eval_jaxpr/while/body/eval_jaxpr/rd,kd->rk/dot_general | solution.py:22
  151.5 10.4 %while.35 = (s32[]{:T(128)}, bf16[2,832,128]{2,1,0:T(8,128)(2,1)S(1)}, bf16[2,832,128]{2,1,0:T(8,128)(2,1)S(1)}, bf16[2128,128]{1,0:T(8,128)(2,1)}, bf16[2128,12...) while((s32[]{:T(128)}, bf16[2,832,128]{2,1,0:T(8,128)(2,1)S(1)}, ...), condition=%wide.region_11.11_spmd.clone, body=%wide.region_8.10_spmd.clone.sunk | while | flops 920869248 | bytes 22954388 | solution.py:110
  151.6 2.7 %fusion.95 = (f32[832]{0:T(1024)S(1)}, f32[832,2128]{1,0:T(8,128)S(1)}) fusion(bf16[2128,128]{1,0:T(8,128)(2,1)} %get-tuple-element.478, bf16[2,832,128]{2,1,0:T(8,128)(2,1)S(1)} %get-tuple-element.477, s32[]{:T(128)} %get-tuple-element.468, s32[832]{0:T(1024)S(1)} %le.126), kind=kOutput, calls=%fused_computation.109.clone.1 | convolution fusion | flops 460328128 | bytes 7847172 | tf_op jit(solution)/shard_map/while/body/eval_jaxpr/while/body/eval_jaxpr/rd,kd->rk/dot_general | solution.py:22
  155.4 1.3 fusion.97
  156.8 2.7 %fusion.95 = (f32[832]{0:T(1024)S(1)}, f32[832,2128]{1,0:T(8,128)S(1)}) fusion(bf16[2128,128]{1,0:T(8,128)(2,1)} %get-tuple-element.478, bf16[2,832,128]{2,1,0:T(8,128)(2,1)S(1)} %get-tuple-element.477, s32[]{:T(128)} %get-tuple-element.468, s32[832]{0:T(1024)S(1)} %le.126), kind=kOutput, calls=%fused_computation.109.clone.1 | convolution fusion | flops 460328128 | bytes 7847172 | tf_op jit(solution)/shard_map/while/body/eval_jaxpr/while/body/eval_jaxpr/rd,kd->rk/dot_general | solution.py:22
  166.7 1.7 dynamic-slice_bitcast_fusion.5
  174.9 10.3 %while.36 = (s32[]{:T(128)}, bf16[2,832,128]{2,1,0:T(8,128)(2,1)S(1)}, bf16[2,832,128]{2,1,0:T(8,128)(2,1)S(1)}, bf16[2128,128]{1,0:T(8,128)(2,1)}, bf16[2128,12...) while((s32[]{:T(128)}, bf16[2,832,128]{2,1,0:T(8,128)(2,1)S(1)}, ...), condition=%wide.region_7.7_spmd.clone, body=%wide.region_4.6_spmd.clone.sunk | while | flops 920869248 | bytes 22954388 | solution.py:110
  175.0 2.6 %fusion.101 = (f32[832]{0:T(1024)S(1)}, f32[832,2128]{1,0:T(8,128)S(1)}) fusion(bf16[2128,128]{1,0:T(8,128)(2,1)} %get-tuple-element.499, bf16[2,832,128]{2,1,0:T(8,128)(2,1)S(1)} %get-tuple-element.498, s32[]{:T(128)} %get-tuple-element.489, s32[832]{0:T(1024)S(1)} %le.127), kind=kOutput, calls=%fused_computation.108.clone.1 | convolution fusion | flops 460328128 | bytes 7847172 | tf_op jit(solution)/shard_map/while/body/eval_jaxpr/while/body/eval_jaxpr/rd,kd->rk/dot_general | solution.py:22
  180.1 2.6 %fusion.101 = (f32[832]{0:T(1024)S(1)}, f32[832,2128]{1,0:T(8,128)S(1)}) fusion(bf16[2128,128]{1,0:T(8,128)(2,1)} %get-tuple-element.499, bf16[2,832,128]{2,1,0:T(8,128)(2,1)S(1)} %get-tuple-element.498, s32[]{:T(128)} %get-tuple-element.489, s32[832]{0:T(1024)S(1)} %le.127), kind=kOutput, calls=%fused_computation.108.clone.1 | convolution fusion | flops 460328128 | bytes 7847172 | tf_op jit(solution)/shard_map/while/body/eval_jaxpr/while/body/eval_jaxpr/rd,kd->rk/dot_general | solution.py:22
  186.7 10.4 %while.35 = (s32[]{:T(128)}, bf16[2,832,128]{2,1,0:T(8,128)(2,1)S(1)}, bf16[2,832,128]{2,1,0:T(8,128)(2,1)S(1)}, bf16[2128,128]{1,0:T(8,128)(2,1)}, bf16[2128,12...) while((s32[]{:T(128)}, bf16[2,832,128]{2,1,0:T(8,128)(2,1)S(1)}, ...), condition=%wide.region_11.11_spmd.clone, body=%wide.region_8.10_spmd.clone.sunk | while | flops 920869248 | bytes 22954388 | solution.py:110
  186.8 2.7 %fusion.95 = (f32[832]{0:T(1024)S(1)}, f32[832,2128]{1,0:T(8,128)S(1)}) fusion(bf16[2128,128]{1,0:T(8,128)(2,1)} %get-tuple-element.478, bf16[2,832,128]{2,1,0:T(8,128)(2,1)S(1)} %get-tuple-element.477, s32[]{:T(128)} %get-tuple-element.468, s32[832]{0:T(1024)S(1)} %le.126), kind=kOutput, calls=%fused_computation.109.clone.1 | convolution fusion | flops 460328128 | bytes 7847172 | tf_op jit(solution)/shard_map/while/body/eval_jaxpr/while/body/eval_jaxpr/rd,kd->rk/dot_general | solution.py:22
  192.0 2.7 %fusion.95 = (f32[832]{0:T(1024)S(1)}, f32[832,2128]{1,0:T(8,128)S(1)}) fusion(bf16[2128,128]{1,0:T(8,128)(2,1)} %get-tuple-element.478, bf16[2,832,128]{2,1,0:T(8,128)(2,1)S(1)} %get-tuple-element.477, s32[]{:T(128)} %get-tuple-element.468, s32[832]{0:T(1024)S(1)} %le.126), kind=kOutput, calls=%fused_computation.109.clone.1 | convolution fusion | flops 460328128 | bytes 7847172 | tf_op jit(solution)/shard_map/while/body/eval_jaxpr/while/body/eval_jaxpr/rd,kd->rk/dot_general | solution.py:22
  (136 shorter events, 45.4 us)
Async XLA Ops:
  0.0 15.4 %copy-start = (bf16[4,256,512]{2,1,0:T(8,128)(2,1)S(1)}, bf16[4,256,512]{2,1,0:T(8,128)(2,1)}, u32[]{:S(2)}) copy-start(bf16[4,256,512]{2,1,0:T(8,128)(2,1)} %param.17) | copy-start | bytes 3145732
  24.6 4.9 %copy-start.3 = (s32[2,8]{1,0:T(2,128)S(1)}, s32[2,8]{1,0:T(2,128)}, u32[]{:S(2)}) copy-start(s32[2,8]{1,0:T(2,128)} %param.19) | copy-start | bytes 196
  24.6 5.1 %copy-start.2 = (s32[32]{0:T(128)S(1)}, s32[32]{0:T(128)}, u32[]{:S(2)}) copy-start(s32[32]{0:T(128)} %param.21) | copy-start | bytes 388
  24.6 98.7 %all-to-all-start = ((bf16[8,2,2,256,256]{4,3,1,2,0:T(8,128)(2,1)}), bf16[8,2,2,256,256]{4,3,1,2,0:T(8,128)(2,1)}, u32[]{:S(2)}, u32[]{:S(2)}) async-start(bf16[8,2,2,256,256]{4,3,1,2,0:T(8,128)(2,1)} %copy.98), calls=%async_computation | async-start | bytes 8388608 | tf_op jit(solution)/shard_map/all_to_all | solution.py:64
  30.5 97.7 %copy-start.4 = (s32[2,1]{0,1:T(1,128)S(1)}, s32[2,1]{0,1:T(1,128)}, u32[]{:S(2)}) copy-start(s32[2,1]{0,1:T(1,128)} %param.20) | copy-start | bytes 28
  198.7 1.2 copy-start.1
where the time goes:
time: 201 us; the launch traced here: 200 us
  waiting for transfers between devices  92.7 us (46%)
  local copies, waits for them, and re-layouts  38.9 us (19%)
  matrix products  31.6 us (16%)
  other arithmetic  14.8 us (7%)
  blocking collectives  13 us (6%)
  starting transfers between devices  4.86 us (2%)
  loops' own time  4.04 us (2%)
    all_to_all x1, waiting for transfers between devices, on_device(): lax.all_to_all(outgoing.reshape(owner_total, slot_room, 2, pass_len, kv_w...  92.7 us
    dot_general x8, matrix products, attend_block(): jnp.einsum('rd,kd->rk', query_rows, key_rows, preferred_element_type=jnp....  21.3 us
    all_gather x1, blocking collectives, on_device(): lax.all_gather(request_pass, 'cache', axis=0, tiled=True)  13 us
    dot_general x8, matrix products, attend_block(): jnp.dot(weights.astype(jnp.bfloat16), value_rows, preferred_element_type=...  10.3 us
    reduce_sum x8, other arithmetic, attend_block(): totals = jnp.sum(weights, axis=1, keepdims=True)  8.91 us
    while x20, local copies, waits for them, and re-layouts  8.91 us
    gather x1, local copies, waits for them, and re-layouts, on_device(): arrived[source_owner, source_rank]  4.93 us
    all_to_all x1, starting transfers between devices, on_device(): lax.all_to_all(outgoing.reshape(owner_total, slot_room, 2, pass_len, kv_w...  4.86 us
  transfers between devices with their start and end apart: 1, of which 1 were waited for; matrix products, arithmetic and copies ran while one was open for 1% of the time, Pallas kernels for 0%

commit v1 on v0

v1 whole, which is shorter than its diff:
```python
import functools
import math

import jax
import jax.numpy as jnp
from jax import lax
from jax.experimental import pallas as pl
from jax.experimental.pallas import tpu as pltpu
from jax.sharding import PartitionSpec as P

HD = 128
BLOCK = 128
MESH = pl.DeviceIdType.MESH
F32 = jnp.float32


def flip(index, step, count):
    total = 0
    bit = 1
    while bit < count:
        total = total + bit * ((index // bit + step // bit) % 2)
        bit *= 2
    return total


def nt_dot(a, b):
    return lax.dot_general(a, b, (((1,), (1,)), ((), ())), preferred_element_type=F32)


def kernel(
    dims,
    q_hbm,
    nk_hbm,
    nv_hbm,
    ck_hbm,
    cv_hbm,
    rp_ref,
    rb_ref,
    ps_ref,
    out_ref,
    q_v,
    nk_v,
    nv_v,
    ck_v,
    cv_v,
    lists,
    jtab,
    send,
    kvbuf,
    qarr,
    m_ref,
    l_ref,
    acc_ref,
    in_sem,
    list_send,
    list_recv,
    send_sem,
    recv_sem,
):
    cache_n, pair_n, reqs, per_req, rooms, pass_dev, pass_len, kvw, rows = dims
    heads = kvw // HD
    group = q_hbm.shape[1] // kvw
    quest = rows - BLOCK
    rec_lanes = group * BLOCK
    lanes = group * rows
    refs = reqs * per_req
    gain = math.log2(math.e) / math.sqrt(HD)
    zc = lax.axis_index("cache")
    zp = lax.axis_index("pair")
    me = zc * pair_n + zp

    loads = [
        pltpu.make_async_copy(src, dst, in_sem.at[i])
        for i, (src, dst) in enumerate(
            ((ck_hbm, ck_v), (cv_hbm, cv_v), (q_hbm, q_v), (nk_hbm, nk_v), (nv_hbm, nv_v))
        )
    ]
    for load in loads:
        load.start()

    barrier = pltpu.get_barrier_semaphore()

    def greet(step, _):
        peer = flip(zc, step // pair_n, cache_n)
        core = (zp + step) % pair_n
        pl.semaphore_signal(
            barrier, inc=1, device_id={"cache": peer, "pair": core}, device_id_type=MESH
        )
        return 0

    lax.fori_loop(1, cache_n * pair_n, greet, 0)
    pl.semaphore_wait(barrier, cache_n * pair_n - 1)

    def list_copy(step, index):
        peer = flip(zc, step, cache_n)
        return pltpu.make_async_remote_copy(
            src_ref=rp_ref,
            dst_ref=lists.at[index],
            send_sem=list_send.at[step],
            recv_sem=list_recv.at[index],
            device_id={"cache": peer, "pair": zp},
            device_id_type=MESH,
        )

    def list_start(step, _):
        list_copy(step, zc).start()
        return 0

    lax.fori_loop(1, cache_n, list_start, 0)
    for load in loads[:2]:
        load.wait()

    def picks(slot_of):
        count = jnp.int32(0)
        chosen = [jnp.int32(0)] * rooms
        for j in range(refs):
            slot = slot_of(j)
            match = slot // pass_dev == me
            for r in range(rooms):
                chosen[r] = jnp.where(match & (count == r), slot % pass_dev, chosen[r])
            count = count + match.astype(jnp.int32)
        return chosen

    def data_copy(step, peer, core, r):
        return pltpu.make_async_remote_copy(
            src_ref=send.at[step, core, r],
            dst_ref=kvbuf.at[me, r],
            send_sem=send_sem.at[step, core, r],
            recv_sem=recv_sem.at[me, r],
            device_id={"cache": peer, "pair": core},
            device_id_type=MESH,
        )

    def fill(dst, pick, core):
        span = pl.ds(pl.multiple_of(core * kvw, kvw), kvw)
        dst[0] = ck_v[pick, :, span]
        dst[1] = cv_v[pick, :, span]

    own = picks(lambda j: ps_ref[rp_ref[j // per_req, j % per_req]])

    def send_step(step):
        peer = flip(zc, step, cache_n)
        list_copy(step, peer).wait_recv()
        chosen = picks(lambda j: ps_ref[lists[peer, j // per_req, j % per_req]])
        for r in range(rooms):
            for core in range(pair_n):
                fill(send.at[step, core, r], chosen[r], core)
                data_copy(step, peer, core, r).start()

    if cache_n == 4:
        for step in (2, 3, 1):
            send_step(step)
    else:
        lax.fori_loop(1, cache_n, lambda step, _: (send_step(step), 0)[1], 0)

    for r in range(rooms):
        for away in range(1, pair_n):
            core = (zp + away) % pair_n
            fill(send.at[0, core, r], own[r], core)
            data_copy(0, zc, core, r).start()
        fill(kvbuf.at[me, r], own[r], zp)

    def seek(owner, _):
        count = jnp.int32(0)
        found = [jnp.int32(-1)] * rooms
        for j in range(refs):
            match = ps_ref[rp_ref[j // per_req, j % per_req]] // pass_dev == owner
            for r in range(rooms):
                found[r] = jnp.where(match & (count == r), j, found[r])
            count = count + match.astype(jnp.int32)
        for r in range(rooms):
            jtab[owner * rooms + r] = found[r]
        return 0

    lax.fori_loop(0, cache_n * pair_n, seek, 0)

    for load in loads[2:]:
        load.wait()
    for i in range(reqs):
        for g in range(heads):
            for h in range(group):
                col = pl.ds((g * group + h) * HD, HD)
                qarr[i, g, pl.ds(h * BLOCK, BLOCK)] = q_v[pl.ds(i * rows, BLOCK), col]
                qarr[i, g, pl.ds(rec_lanes + h * quest, quest)] = q_v[
                    pl.ds(i * rows + BLOCK, quest), col
                ]

    tiles = []
    for start, stop in ((0, rec_lanes), (rec_lanes, lanes)):
        at = start
        while at < stop:
            width = min(256, stop - at)
            tiles.append((at, width))
            at += width

    for i in range(reqs):
        for g in range(heads):
            col = pl.ds(g * HD, HD)
            for at, width in tiles:
                depth = BLOCK if at < rec_lanes else rows
                keys = nk_v[pl.ds(i * rows, depth), col]
                values = nv_v[pl.ds(i * rows, depth), col]
                scores = nt_dot(keys, qarr[i, g, pl.ds(at, width)])
                key_row = lax.broadcasted_iota(jnp.int32, (depth, width), 0)
                lane = lax.broadcasted_iota(jnp.int32, (depth, width), 1)
                if at < rec_lanes:
                    own_row = (lane + at) % BLOCK
                else:
                    own_row = (lane + (at - rec_lanes)) % quest + BLOCK
                scores = jnp.where(key_row <= own_row, scores, -jnp.inf)
                top = jnp.max(scores, axis=0, keepdims=True)
                weights = jnp.exp2(scores * gain - top * gain)
                m_ref[i, g, :, pl.ds(at, width)] = top
                l_ref[i, g, :, pl.ds(at, width)] = jnp.sum(weights, axis=0, keepdims=True)
                acc_ref[i, g, :, pl.ds(at, width)] = jnp.dot(
                    values.T, weights.astype(jnp.bfloat16), preferred_element_type=F32
                )

    def chunk(owner, r):
        j = jtab[owner * rooms + r]
        valid = j >= 0
        j = jnp.maximum(j, 0)
        req = j // per_req
        blocks = pass_len // BLOCK
        first = (j % per_req) * blocks
        fresh = rb_ref[req, 0]
        shown = [
            (valid & (first + b < fresh), valid & (first + b != fresh)) for b in range(blocks)
        ]
        for g in range(heads):
            col = pl.ds(g * HD, HD)
            keys = kvbuf[owner, r, 0, :, col]
            values_t = kvbuf[owner, r, 1, :, col].T
            for at, width in tiles:
                kind = 0 if at < rec_lanes else 1
                span = pl.ds(at, width)
                scores = nt_dot(keys, qarr[req, g, span])
                old_top = m_ref[req, g, :, span]
                top = old_top
                for b in range(blocks):
                    part = jnp.max(scores[b * BLOCK : (b + 1) * BLOCK], axis=0, keepdims=True)
                    top = jnp.maximum(top, jnp.where(shown[b][kind], part, -jnp.inf))
                scaled = top * gain
                pieces = []
                total = jnp.zeros_like(top)
                for b in range(blocks):
                    shift = jnp.where(shown[b][kind], scaled, jnp.inf)
                    piece = jnp.exp2(scores[b * BLOCK : (b + 1) * BLOCK] * gain - shift)
                    total = total + jnp.sum(piece, axis=0, keepdims=True)
                    pieces.append(piece.astype(jnp.bfloat16))
                weights = jnp.concatenate(pieces, axis=0)
                decay = jnp.exp2(old_top * gain - scaled)
                total = l_ref[req, g, :, span] * decay + total
                mixed = jnp.dot(values_t, weights, preferred_element_type=F32)
                mixed = acc_ref[req, g, :, span] * decay + mixed
                for i in range(reqs):
                    mine = req == i
                    m_ref[i, g, :, span] = jnp.where(mine, top, m_ref[i, g, :, span])
                    l_ref[i, g, :, span] = jnp.where(mine, total, l_ref[i, g, :, span])
                    acc_ref[i, g, :, span] = jnp.where(mine, mixed, acc_ref[i, g, :, span])

    for r in range(rooms):
        chunk(me, r)

    def arrive(step, core, r):
        owner = flip(zc, step, cache_n) * pair_n + core
        pltpu.make_async_remote_copy(
            src_ref=send.at[0, 0, r],
            dst_ref=kvbuf.at[owner, r],
            send_sem=send_sem.at[0, 0, r],
            recv_sem=recv_sem.at[owner, r],
            device_id={"cache": owner // pair_n, "pair": core},
            device_id_type=MESH,
        ).wait_recv()
        chunk(owner, r)

    for away in range(1, pair_n):
        for r in range(rooms):
            arrive(0, (zp + away) % pair_n, r)

    def take(t, _):
        step = t // (rooms * pair_n)
        if cache_n == 4:
            step = 2 + step - 3 * (step // 2)
        else:
            step = step + 1
        arrive(step, t % pair_n, t // pair_n % rooms)
        return 0

    lax.fori_loop(0, (cache_n - 1) * rooms * pair_n, take, 0)

    for i in range(reqs):
        for g in range(heads):
            for h in range(group):
                span = pl.ds(h * BLOCK, BLOCK)
                done = acc_ref[i, g, :, span] / l_ref[i, g, :, span]
                out_ref[pl.ds(i * rows, BLOCK), pl.ds((g * group + h) * HD, HD)] = done.T.astype(
                    out_ref.dtype
                )
            span = pl.ds(rec_lanes, lanes - rec_lanes)
            done = (acc_ref[i, g, :, span] / l_ref[i, g, :, span]).T.astype(out_ref.dtype)
            for h in range(group):
                out_ref[pl.ds(i * rows + BLOCK, quest), pl.ds((g * group + h) * HD, HD)] = done[
                    h * quest : (h + 1) * quest
                ]

    def list_end(step, _):
        list_copy(step, zc).wait_send()
        return 0

    lax.fori_loop(1, cache_n, list_end, 0)

    def data_end(step, _):
        for core in range(pair_n):
            for r in range(rooms):
                data_copy(step, zc, core, r).wait_send()
        return 0

    lax.fori_loop(1, cache_n, data_end, 0)
    for away in range(1, pair_n):
        for r in range(rooms):
            data_copy(0, zc, (zp + away) % pair_n, r).wait_send()


def on_device(
    queries, new_keys, new_values, cache_keys, cache_values, request_pass, rec_block, passage_slot
):
    reqs, per_req = request_pass.shape
    cache_n = lax.axis_size("cache")
    pair_n = lax.axis_size("pair")
    owners = cache_n * pair_n
    rooms = max(1, (reqs * per_req + owners - 1) // owners)
    pass_dev, pass_len, cache_width = cache_keys.shape
    kvw = cache_width // pair_n
    rows = queries.shape[0] // reqs
    heads = kvw // HD
    lanes = queries.shape[1] // kvw * rows
    dims = (cache_n, pair_n, reqs, per_req, rooms, pass_dev, pass_len, kvw, rows)
    bf16 = jnp.bfloat16
    hbm = pl.BlockSpec(memory_space=pl.ANY)
    smem = pl.BlockSpec(memory_space=pltpu.SMEM)
    return pl.pallas_call(
        functools.partial(kernel, dims),
        out_shape=jax.ShapeDtypeStruct(queries.shape, bf16),
        in_specs=[hbm] * 5 + [smem] * 3,
        out_specs=pl.BlockSpec(memory_space=pltpu.VMEM),
        scratch_shapes=[
            pltpu.VMEM(queries.shape, bf16),
            pltpu.VMEM(new_keys.shape, bf16),
            pltpu.VMEM(new_values.shape, bf16),
            pltpu.VMEM(cache_keys.shape, bf16),
            pltpu.VMEM(cache_values.shape, bf16),
            pltpu.SMEM((cache_n, reqs, per_req), jnp.int32),
            pltpu.SMEM((owners * rooms,), jnp.int32),
            pltpu.VMEM((cache_n, pair_n, rooms, 2, pass_len, kvw), bf16),
            pltpu.VMEM((owners, rooms, 2, pass_len, kvw), bf16),
            pltpu.VMEM((reqs, heads, lanes, HD), bf16),
            pltpu.VMEM((reqs, heads, 1, lanes), F32),
            pltpu.VMEM((reqs, heads, 1, lanes), F32),
            pltpu.VMEM((reqs, heads, HD, lanes), F32),
            pltpu.SemaphoreType.DMA((5,)),
            pltpu.SemaphoreType.DMA((cache_n,)),
            pltpu.SemaphoreType.DMA((cache_n,)),
            pltpu.SemaphoreType.DMA((cache_n, pair_n, rooms)),
            pltpu.SemaphoreType.DMA((owners, rooms)),
        ],
        compiler_params=pltpu.CompilerParams(
            collective_id=0, has_side_effects=True, vmem_limit_bytes=48 * 1024 * 1024
        ),
    )(
        queries,
        new_keys,
        new_values,
        cache_keys,
        cache_values,
        request_pass,
        rec_block,
        passage_slot,
    )


def solution(mesh):
    return jax.shard_map(
        on_device,
        mesh=mesh,
        in_specs=(
            P(("groups", "cache"), ("heads", "pair")),
            P(("groups", "cache"), ("heads", "pair")),
            P(("groups", "cache"), ("heads", "pair")),
            P(("groups", "cache", "pair"), None, "heads"),
            P(("groups", "cache", "pair"), None, "heads"),
            P(("groups", "cache"), None),
            P(("groups", "cache"), None),
            P("groups"),
        ),
        out_specs=P(("groups", "cache"), ("heads", "pair")),
        check_vma=False,
    )
```

time: 201 us -> 132 us (0.66)
  the two profiles are of different devices: /device:TPU:0 before, /device:TPU:15 now
where the time goes in v1:
time: 132 us
  Pallas kernels  123 us (93%)
  local copies, waits for them, and re-layouts  9.03 us (7%)
    pallas_call x1, Pallas kernels, on_device(): pl.pallas_call(functools.partial(kernel, dims), out_shape=jax.ShapeDtypeS...  123 us
    unnamed x16, local copies, waits for them, and re-layouts  9.03 us

profile of v1, /device:TPU:15, one launch (start us, length us, event | category | flops | bytes accessed | tf_op | source)
XLA Modules:
  0.0 132.1 jit_solution(2506594106723393204)
XLA Ops:
  0.0 0.7 copy.9.rb_ref
  0.7 0.0 copy-start
  0.7 1.5 %copy-done = bf16[416,2048]{1,0:T(8,128)(2,1)S(1)} copy-done((bf16[416,2048]{1,0:T(8,128)(2,1)S(1)}, bf16[416,2048]{1,0:T(8,128)(2,1)}, u32[]{:S(2)}) %copy-start) | copy-done | bytes 1703960
  2.2 0.0 copy-start.1
  2.2 1.2 copy-done.1
  3.4 0.0 copy-start.2
  3.4 1.2 copy-done.2
  4.6 0.0 copy-start.3
  4.6 0.9 copy-done.3
  5.6 0.0 copy-start.4
  5.6 0.9 copy-done.4
  6.5 0.0 copy-start.5
  6.5 0.7 copy-done.5
  7.2 0.0 copy-start.6
  7.2 0.7 copy-done.6
  7.8 123.1 %shard_map.82 = bf16[416,2048]{1,0:T(8,128)(2,1)S(1)} custom-call(bf16[416,2048]{1,0:T(8,128)(2,1)S(1)} %copy-done, bf16[416,256]{1,0:T(8,128)(2,1)S(1)} %copy-done.3, bf16[416,256]{1,0:T(8,128)(2,1)S(1)} %copy-done.4, bf16[4,256,512]{2,1,0:T(8,128)(2,1)S(1)} %copy-done.1, bf16[4,256,512]{2,1,0:T(8,128)(2,1)S(1)} %copy-done.2, s32[2,8]{1,0:T(2,128)S(1)} %copy-done.5, ...), custom_call_target="tpu_custom_call" | custom-call | tf_op jit(solution)/shard_map/pallas_call | solution.py:342
  131.0 1.2 copy.11
Async XLA Ops:
  0.7 1.5 %copy-start = (bf16[416,2048]{1,0:T(8,128)(2,1)S(1)}, bf16[416,2048]{1,0:T(8,128)(2,1)}, u32[]{:S(2)}) copy-start(bf16[416,2048]{1,0:T(8,128)(2,1)} %q_hbm.1) | copy-start | bytes 5111812
  2.2 1.2 copy-start.1
  3.4 1.2 copy-start.2
  4.6 0.9 copy-start.3
  5.6 0.9 copy-start.4
  6.5 0.7 copy-start.5
  7.2 0.7 copy-start.6

commit v2 on v1

--- a/solution.py
+++ b/solution.py
@@ -200,20 +200,21 @@
                 depth = BLOCK if at < rec_lanes else rows
                 keys = nk_v[pl.ds(i * rows, depth), col]
                 values = nv_v[pl.ds(i * rows, depth), col]
-                scores = nt_dot(keys, qarr[i, g, pl.ds(at, width)])
-                key_row = lax.broadcasted_iota(jnp.int32, (depth, width), 0)
-                lane = lax.broadcasted_iota(jnp.int32, (depth, width), 1)
+                scores = nt_dot(qarr[i, g, pl.ds(at, width)], keys)
+                key_row = lax.broadcasted_iota(jnp.int32, (width, depth), 1)
+                lane = lax.broadcasted_iota(jnp.int32, (width, depth), 0)
                 if at < rec_lanes:
                     own_row = (lane + at) % BLOCK
                 else:
                     own_row = (lane + (at - rec_lanes)) % quest + BLOCK
                 scores = jnp.where(key_row <= own_row, scores, -jnp.inf)
-                top = jnp.max(scores, axis=0, keepdims=True)
+                top = jnp.max(scores, axis=1, keepdims=True)
                 weights = jnp.exp2(scores * gain - top * gain)
-                m_ref[i, g, :, pl.ds(at, width)] = top
-                l_ref[i, g, :, pl.ds(at, width)] = jnp.sum(weights, axis=0, keepdims=True)
-                acc_ref[i, g, :, pl.ds(at, width)] = jnp.dot(
-                    values.T, weights.astype(jnp.bfloat16), preferred_element_type=F32
+                total = jnp.sum(weights, axis=1, keepdims=True) * (1.0 / HD)
+                m_ref[i, g, pl.ds(at, width)] = jnp.broadcast_to(top, (width, HD))
+                l_ref[i, g, pl.ds(at, width)] = jnp.broadcast_to(total, (width, HD))
+                acc_ref[i, g, pl.ds(at, width)] = jnp.dot(
+                    weights.astype(jnp.bfloat16), values, preferred_element_type=F32
                 )
 
     def chunk(owner, r):
@@ -230,34 +231,34 @@
         for g in range(heads):
             col = pl.ds(g * HD, HD)
             keys = kvbuf[owner, r, 0, :, col]
-            values_t = kvbuf[owner, r, 1, :, col].T
+            values = kvbuf[owner, r, 1, :, col]
             for at, width in tiles:
                 kind = 0 if at < rec_lanes else 1
                 span = pl.ds(at, width)
-                scores = nt_dot(keys, qarr[req, g, span])
-                old_top = m_ref[req, g, :, span]
-                top = old_top
-                for b in range(blocks):
-                    part = jnp.max(scores[b * BLOCK : (b + 1) * BLOCK], axis=0, keepdims=True)
-                    top = jnp.maximum(top, jnp.where(shown[b][kind], part, -jnp.inf))
+                scores = nt_dot(qarr[req, g, span], keys)
+                parts = [scores[:, b * BLOCK : (b + 1) * BLOCK] for b in range(blocks)]
+                best = jnp.where(shown[0][kind], parts[0], -jnp.inf)
+                for b in range(1, blocks):
+                    best = jnp.maximum(best, jnp.where(shown[b][kind], parts[b], -jnp.inf))
+                old_top = m_ref[req, g, span]
+                top = jnp.maximum(old_top, jnp.max(best, axis=1, keepdims=True))
                 scaled = top * gain
                 pieces = []
-                total = jnp.zeros_like(top)
+                decay = jnp.exp2(old_top * gain - scaled)
+                total = l_ref[req, g, span] * decay
                 for b in range(blocks):
                     shift = jnp.where(shown[b][kind], scaled, jnp.inf)
-                    piece = jnp.exp2(scores[b * BLOCK : (b + 1) * BLOCK] * gain - shift)
-                    total = total + jnp.sum(piece, axis=0, keepdims=True)
+                    piece = jnp.exp2(parts[b] * gain - shift)
+                    total = total + piece
                     pieces.append(piece.astype(jnp.bfloat16))
-                weights = jnp.concatenate(pieces, axis=0)
-                decay = jnp.exp2(old_top * gain - scaled)
-                total = l_ref[req, g, :, span] * decay + total
-                mixed = jnp.dot(values_t, weights, preferred_element_type=F32)
-                mixed = acc_ref[req, g, :, span] * decay + mixed
+                weights = jnp.concatenate(pieces, axis=1)
+                mixed = jnp.dot(weights, values, preferred_element_type=F32)
+                mixed = acc_ref[req, g, span] * decay + mixed
                 for i in range(reqs):
                     mine = req == i
-                    m_ref[i, g, :, span] = jnp.where(mine, top, m_ref[i, g, :, span])
-                    l_ref[i, g, :, span] = jnp.where(mine, total, l_ref[i, g, :, span])
-                    acc_ref[i, g, :, span] = jnp.where(mine, mixed, acc_ref[i, g, :, span])
+                    m_ref[i, g, span] = jnp.where(mine, top, m_ref[i, g, span])
+                    l_ref[i, g, span] = jnp.where(mine, total, l_ref[i, g, span])
+                    acc_ref[i, g, span] = jnp.where(mine, mixed, acc_ref[i, g, span])
 
     for r in range(rooms):
         chunk(me, r)
@@ -292,17 +293,16 @@
     for i in range(reqs):
         for g in range(heads):
             for h in range(group):
-                span = pl.ds(h * BLOCK, BLOCK)
-                done = acc_ref[i, g, :, span] / l_ref[i, g, :, span]
-                out_ref[pl.ds(i * rows, BLOCK), pl.ds((g * group + h) * HD, HD)] = done.T.astype(
-                    out_ref.dtype
-                )
-            span = pl.ds(rec_lanes, lanes - rec_lanes)
-            done = (acc_ref[i, g, :, span] / l_ref[i, g, :, span]).T.astype(out_ref.dtype)
-            for h in range(group):
-                out_ref[pl.ds(i * rows + BLOCK, quest), pl.ds((g * group + h) * HD, HD)] = done[
-                    h * quest : (h + 1) * quest
-                ]
+                col = pl.ds((g * group + h) * HD, HD)
+                for at, to, size in (
+                    (h * BLOCK, i * rows, BLOCK),
+                    (rec_lanes + h * quest, i * rows + BLOCK, quest),
+                ):
+                    span = pl.ds(at, size)
+                    total = jnp.sum(l_ref[i, g, span], axis=1, keepdims=True)
+                    out_ref[pl.ds(to, size), col] = (acc_ref[i, g, span] / total).astype(
+                        out_ref.dtype
+                    )
 
     def list_end(step, _):
         list_copy(step, zc).wait_send()
@@ -355,9 +355,9 @@
             pltpu.VMEM((cache_n, pair_n, rooms, 2, pass_len, kvw), bf16),
             pltpu.VMEM((owners, rooms, 2, pass_len, kvw), bf16),
             pltpu.VMEM((reqs, heads, lanes, HD), bf16),
-            pltpu.VMEM((reqs, heads, 1, lanes), F32),
-            pltpu.VMEM((reqs, heads, 1, lanes), F32),
-            pltpu.VMEM((reqs, heads, HD, lanes), F32),
+            pltpu.VMEM((reqs, heads, lanes, HD), F32),
+            pltpu.VMEM((reqs, heads, lanes, HD), F32),
+            pltpu.VMEM((reqs, heads, lanes, HD), F32),
             pltpu.SemaphoreType.DMA((5,)),
             pltpu.SemaphoreType.DMA((cache_n,)),
             pltpu.SemaphoreType.DMA((cache_n,)),

time: 132 us -> 124 us (0.939)
  Pallas kernels: 123 us -> 115 us
    pallas_call x1, Pallas kernels: 123 us -> 115 us  [on_device(): pl.pallas_call(functools.partial(kernel, dims), out_shape=jax.ShapeDtypeS...]
where the time goes in v2:
time: 124 us
  Pallas kernels  115 us (93%)
  local copies, waits for them, and re-layouts  9.03 us (7%)
    pallas_call x1, Pallas kernels, on_device(): pl.pallas_call(functools.partial(kernel, dims), out_shape=jax.ShapeDtypeS...  115 us
    unnamed x16, local copies, waits for them, and re-layouts  9.03 us

profile of v2, /device:TPU:15, one launch (start us, length us, event | category | flops | bytes accessed | tf_op | source)
XLA Modules:
  0.0 124.1 jit_solution(5090191028759000061)
XLA Ops:
  0.0 0.7 copy.9.rb_ref
  0.7 0.0 copy-start
  0.7 1.5 %copy-done = bf16[416,2048]{1,0:T(8,128)(2,1)S(1)} copy-done((bf16[416,2048]{1,0:T(8,128)(2,1)S(1)}, bf16[416,2048]{1,0:T(8,128)(2,1)}, u32[]{:S(2)}) %copy-start) | copy-done | bytes 1703960
  2.2 0.0 copy-start.1
  2.2 1.2 copy-done.1
  3.4 0.0 copy-start.2
  3.4 1.2 copy-done.2
  4.6 0.0 copy-start.3
  4.6 0.9 copy-done.3
  5.6 0.0 copy-start.4
  5.6 0.9 copy-done.4
  6.5 0.0 copy-start.5
  6.5 0.7 copy-done.5
  7.2 0.0 copy-start.6
  7.2 0.7 copy-done.6
  7.8 115.1 %shard_map.82 = bf16[416,2048]{1,0:T(8,128)(2,1)S(1)} custom-call(bf16[416,2048]{1,0:T(8,128)(2,1)S(1)} %copy-done, bf16[416,256]{1,0:T(8,128)(2,1)S(1)} %copy-done.3, bf16[416,256]{1,0:T(8,128)(2,1)S(1)} %copy-done.4, bf16[4,256,512]{2,1,0:T(8,128)(2,1)S(1)} %copy-done.1, bf16[4,256,512]{2,1,0:T(8,128)(2,1)S(1)} %copy-done.2, s32[2,8]{1,0:T(2,128)S(1)} %copy-done.5, ...), custom_call_target="tpu_custom_call" | custom-call | tf_op jit(solution)/shard_map/pallas_call | solution.py:342
  123.0 1.2 copy.11
Async XLA Ops:
  0.7 1.5 %copy-start = (bf16[416,2048]{1,0:T(8,128)(2,1)S(1)}, bf16[416,2048]{1,0:T(8,128)(2,1)}, u32[]{:S(2)}) copy-start(bf16[416,2048]{1,0:T(8,128)(2,1)} %q_hbm.1) | copy-start | bytes 5111812
  2.2 1.2 copy-start.1
  3.4 1.2 copy-start.2
  4.6 0.9 copy-start.3
  5.6 0.9 copy-start.4
  6.5 0.7 copy-start.5
  7.2 0.7 copy-start.6

commit v3 on v2

--- a/solution.py
+++ b/solution.py
@@ -148,8 +148,8 @@
                 data_copy(step, peer, core, r).start()
 
     if cache_n == 4:
-        for step in (2, 3, 1):
-            send_step(step)
+        for turn in range(3):
+            send_step((turn + 1 - zp) % 3 + 1)
     else:
         lax.fori_loop(1, cache_n, lambda step, _: (send_step(step), 0)[1], 0)
 
@@ -282,7 +282,7 @@
     def take(t, _):
         step = t // (rooms * pair_n)
         if cache_n == 4:
-            step = 2 + step - 3 * (step // 2)
+            step = (step + 1 - t % pair_n) % 3 + 1
         else:
             step = step + 1
         arrive(step, t % pair_n, t // pair_n % rooms)

time: 124 us -> 125 us (level)
  no operation moved by 1% of the time
where the time goes in v3:
time: 125 us; the launch traced here: 124 us
  Pallas kernels  115 us (92%)
  local copies, waits for them, and re-layouts  9.03 us (7%)
    pallas_call x1, Pallas kernels, on_device(): pl.pallas_call(functools.partial(kernel, dims), out_shape=jax.ShapeDtypeS...  115 us
    unnamed x16, local copies, waits for them, and re-layouts  9.03 us

profile of v3, /device:TPU:15, one launch (start us, length us, event | category | flops | bytes accessed | tf_op | source)
XLA Modules:
  0.0 124.3 jit_solution(10814000901645873858)
XLA Ops:
  0.0 0.7 copy.9.rb_ref
  0.7 0.0 copy-start
  0.7 1.5 %copy-done = bf16[416,2048]{1,0:T(8,128)(2,1)S(1)} copy-done((bf16[416,2048]{1,0:T(8,128)(2,1)S(1)}, bf16[416,2048]{1,0:T(8,128)(2,1)}, u32[]{:S(2)}) %copy-start) | copy-done | bytes 1703960
  2.2 0.0 copy-start.1
  2.2 1.2 copy-done.1
  3.4 0.0 copy-start.2
  3.4 1.2 copy-done.2
  4.6 0.0 copy-start.3
  4.6 0.9 copy-done.3
  5.6 0.0 copy-start.4
  5.6 0.9 copy-done.4
  6.5 0.0 copy-start.5
  6.5 0.7 copy-done.5
  7.2 0.0 copy-start.6
  7.2 0.7 copy-done.6
  7.8 115.2 %shard_map.82 = bf16[416,2048]{1,0:T(8,128)(2,1)S(1)} custom-call(bf16[416,2048]{1,0:T(8,128)(2,1)S(1)} %copy-done, bf16[416,256]{1,0:T(8,128)(2,1)S(1)} %copy-done.3, bf16[416,256]{1,0:T(8,128)(2,1)S(1)} %copy-done.4, bf16[4,256,512]{2,1,0:T(8,128)(2,1)S(1)} %copy-done.1, bf16[4,256,512]{2,1,0:T(8,128)(2,1)S(1)} %copy-done.2, s32[2,8]{1,0:T(2,128)S(1)} %copy-done.5, ...), custom_call_target="tpu_custom_call" | custom-call | tf_op jit(solution)/shard_map/pallas_call | solution.py:342
  123.1 1.2 copy.11
Async XLA Ops:
  0.7 1.5 %copy-start = (bf16[416,2048]{1,0:T(8,128)(2,1)S(1)}, bf16[416,2048]{1,0:T(8,128)(2,1)}, u32[]{:S(2)}) copy-start(bf16[416,2048]{1,0:T(8,128)(2,1)} %q_hbm.1) | copy-start | bytes 5111812
  2.2 1.2 copy-start.1
  3.4 1.2 copy-start.2
  4.6 0.9 copy-start.3
  5.6 0.9 copy-start.4
  6.5 0.7 copy-start.5
  7.2 0.7 copy-start.6
